TPU v7x, 512 devices: a whole 4x4x16 slice. The times are simulated.
512 devices in a mesh: enc: 16 (over x, z_hi), seq: 8 (over y, core), tp: 4 (over z_lo).
Axes of the slice: x: 4, y: 4, z: 16 (z_hi: 4, z_lo: 4; z = z_hi * 4 + z_lo), core: 2. Of those that a mesh axis runs over, the one named last changes fastest.
Arguments:
- visual_key_value: bfloat16 [16, 16, 256, 2048], P(None, 'seq', 'enc', 'tp'), may hold values from -4.5 to 4.5
- patch_blocks: int32 [16, 16], P('enc'), may hold values from 1 to 8
- queries: bfloat16 [16, 16, 32, 8192], P('enc', 'seq', None, 'tp'), may hold values from -113 to 113
- suffix_key_value: bfloat16 [16, 16, 32, 2048], P('enc', 'seq', None, 'tp'), may hold values from -6 to 6
- suffix_hidden_state: bfloat16 [16, 16, 32, 8192], P('enc', 'seq', None, 'tp'), may hold values from -6 to 6
- down_weight: bfloat16 [8192, 128], P('tp'), may hold values from -0.0625 to 0.0625
- up_weight: bfloat16 [128, 8192], P(None, 'tp'), may hold values from -1.5 to 1.5
- question_adapter: int32 [16, 16], P('enc', 'seq'), may hold values from 0 to 7
- suffix_token_length: int32 [16, 16], P('enc', 'seq'), may hold values from 1 to 32
Outputs:
- context: bfloat16 [16, 16, 32, 8192], P('enc', 'seq', None, 'tp')
All inputs are finite; a program needn't handle non-finite values.
Results may differ from a plain program's by a relative error of at most 0.0087.
Values may be sent and summed in bfloat16 or wider, within the bound.
A program may use at most 64 MiB of HBM per device.

v0:
```python
import math

import jax
import jax.numpy as jnp
from jax import lax
from jax.sharding import PartitionSpec as P

HEAD_SIZE = 128
ADAPTER_RANK = 16


NEG_BIG = -1e30
ADAPTER_SCALE = 2.0


def sent_to_all(shard, axis):
    copies = jnp.broadcast_to(shard, (lax.axis_size(axis), *shard.shape))
    return lax.all_to_all(copies, axis, split_axis=0, concat_axis=0, tiled=True)


def over_copies(shard, axis):
    return sent_to_all(shard, axis).sum(axis=0)


def per_device(
    visual_key_value,
    patch_blocks,
    queries,
    suffix_key_value,
    suffix_hidden_state,
    down_weight,
    up_weight,
    question_adapter,
    suffix_token_length,
):
    docs_here, asked_here, suffix_len, query_feature_width = queries.shape
    kv_local = suffix_key_value.shape[3] // (2 * HEAD_SIZE)
    head_group = query_feature_width // (kv_local * HEAD_SIZE)
    asked_rows = asked_here * suffix_len
    row_totals = docs_here * asked_rows
    inverse = 1.0 / math.sqrt(HEAD_SIZE)
    enc_count = lax.axis_size("enc")
    hidden_state_rows = suffix_hidden_state.reshape(row_totals, suffix_hidden_state.shape[3])
    reduced_features = jnp.dot(hidden_state_rows, down_weight, preferred_element_type=jnp.float32)
    owning_question = lax.broadcasted_iota(jnp.int32, (1, down_weight.shape[1]), 1) // ADAPTER_RANK
    row_ids = jnp.broadcast_to(
        question_adapter[:, :, None], (docs_here, asked_here, suffix_len)
    ).reshape(row_totals, 1)
    reduced_features = jnp.where(owning_question == row_ids, reduced_features, 0.0)
    selected_adapter = over_copies(reduced_features, "tp").astype(jnp.bfloat16)
    raised_features = jnp.dot(selected_adapter, up_weight, preferred_element_type=jnp.float32)
    query_matrix = (
        queries.reshape(row_totals, query_feature_width).astype(jnp.float32)
        + ADAPTER_SCALE * raised_features
    ).astype(jnp.bfloat16)
    query_matrix = query_matrix.reshape(docs_here, asked_rows, kv_local, head_group, HEAD_SIZE)
    suffix_pairs = suffix_key_value.reshape(
        docs_here, asked_here, suffix_len, kv_local, 2, HEAD_SIZE
    )
    query_split = query_matrix.reshape(
        docs_here, asked_here, suffix_len, kv_local, head_group, HEAD_SIZE
    )
    suffix_scores = (
        jnp.einsum(
            "bqikgd,bqjkd->bkgqij",
            query_split,
            suffix_pairs[:, :, :, :, 0, :],
            preferred_element_type=jnp.float32,
        )
        * inverse
    )
    positions = lax.broadcasted_iota(jnp.int32, (suffix_len, suffix_len), 0)
    columns = lax.broadcasted_iota(jnp.int32, (suffix_len, suffix_len), 1)
    causal = columns <= positions
    within = (
        lax.broadcasted_iota(jnp.int32, (1, 1, suffix_len), 2) < suffix_token_length[:, :, None]
    )
    suffix_mask = (causal[None, None, :, :] & within[:, :, None, :])[:, None, None]
    suffix_scores = jnp.where(suffix_mask, suffix_scores, NEG_BIG)
    suffix_peak = suffix_scores.max(axis=-1)
    suffix_weights = jnp.where(suffix_mask, jnp.exp(suffix_scores - suffix_peak[..., None]), 0.0)
    running = suffix_peak.reshape(docs_here, kv_local, head_group, asked_rows)
    totals = suffix_weights.sum(axis=-1).reshape(docs_here, kv_local, head_group, asked_rows)
    numerators = jnp.einsum(
        "bkgqij,bqjkd->bkgqid",
        suffix_weights.astype(jnp.bfloat16),
        suffix_pairs[:, :, :, :, 1, :],
        preferred_element_type=jnp.float32,
    )
    numerators = numerators.reshape(docs_here, kv_local, head_group, asked_rows, HEAD_SIZE)
    carried = (running, totals, numerators)
    exchanged = lax.all_to_all(visual_key_value, "enc", split_axis=0, concat_axis=0, tiled=True)
    key_piece = lax.all_gather(exchanged, "seq", axis=1, tiled=True)
    peaks_now, totals_now, numer_now = carried
    tile_rows, page_count, tile_len, piece_width = key_piece.shape
    key_values = key_piece.reshape(enc_count, docs_here, page_count, tile_len, piece_width)
    key_values = jnp.moveaxis(key_values, 1, 0).reshape(
        docs_here, enc_count * page_count * tile_len, kv_local, 2, HEAD_SIZE
    )
    token_pos = lax.broadcasted_iota(
        jnp.int32, (1, enc_count, 1, tile_len), 1
    ) * tile_len + lax.broadcasted_iota(jnp.int32, (1, enc_count, 1, tile_len), 3)
    live_keys = 8 * token_pos < patch_blocks[:, None, :, None] * (enc_count * tile_len)
    live_keys = live_keys.reshape(docs_here, 1, 1, 1, enc_count * page_count * tile_len)
    scores = (
        jnp.einsum(
            "bnkgd,blkd->bkgnl",
            query_matrix,
            key_values[:, :, :, 0, :],
            preferred_element_type=jnp.float32,
        )
        * inverse
    )
    scores = jnp.where(live_keys, scores, NEG_BIG)
    updated = jnp.maximum(peaks_now, scores.max(axis=-1))
    rescale = jnp.exp(peaks_now - updated)
    weights = jnp.where(live_keys, jnp.exp(scores - updated[..., None]), 0.0)
    totals_next = totals_now * rescale + weights.sum(axis=-1)
    numer_next = numer_now * rescale[..., None] + jnp.einsum(
        "bkgnl,blkd->bkgnd",
        weights.astype(jnp.bfloat16),
        key_values[:, :, :, 1, :],
        preferred_element_type=jnp.float32,
    )
    carried = (updated, totals_next, numer_next)
    running, totals, numerators = carried
    context = numerators / totals[..., None]
    context = jnp.transpose(context, (0, 3, 1, 2, 4)).reshape(
        docs_here, asked_here, suffix_len, query_feature_width
    )
    kept_rows = (
        lax.broadcasted_iota(jnp.int32, (1, 1, suffix_len), 2) < suffix_token_length[:, :, None]
    )
    return jnp.where(kept_rows[:, :, :, None], context, 0.0).astype(jnp.bfloat16)


def solution(mesh):
    placed = (
        P(None, "seq", "enc", "tp"),
        P("enc", None),
        P("enc", "seq", None, "tp"),
        P("enc", "seq", None, "tp"),
        P("enc", "seq", None, "tp"),
        P("tp", None),
        P(None, "tp"),
        P("enc", "seq"),
        P("enc", "seq"),
    )
    return jax.shard_map(
        per_device,
        mesh=mesh,
        in_specs=placed,
        out_specs=P("enc", "seq", None, "tp"),
        check_vma=False,
    )
```

profile of v0, /device:TPU:1, one launch (start us, length us, event | category | flops | bytes accessed | tf_op | source)
XLA Modules:
  0.0 128.2 jit_solution(13732557373285925791)
XLA Ops:
  6.5 45.5 %all_to_all.10 = bf16[16,2,16,512]{3,2,1,0:T(8,128)(2,1)} all-to-all(bf16[16,2,16,512]{3,2,1,0:T(8,128)(2,1)} %param.9), channel_id=1, replica_groups=mesh['enc'=16,'seq'=8,'tp'=4] {'enc'}, dimensions={0} | all-to-all | bytes 1048576 | tf_op jit(solution)/shard_map/all_to_all | solution.py:92
  52.1 0.7 broadcast_in_dim.81
  52.9 1.3 %convolution_select_fusion = f32[64,128]{1,0:T(8,128)S(1)} fusion(bf16[64,2048]{1,0:T(8,128)(2,1)} %bitcast.147, bf16[2048,128]{1,0:T(8,128)(2,1)} %param.14, s32[128]{0:T(128)S(1)} %and_select_fusion, s32[64]{0:T(128)S(1)} %broadcast_in_dim.82), kind=kOutput, calls=%fused_computation.24 | convolution fusion | flops 33570816 | bytes 819968 | tf_op jit(solution)/shard_map/dot_general | solution.py:44
  54.3 0.7 broadcast_in_dim.84
  54.9 9.1 %all-to-all-start = ((f32[4,64,128]{2,1,0:T(8,128)}), f32[4,64,128]{2,1,0:T(8,128)S(1)}, u32[]{:S(2)}, u32[]{:S(2)}) async-start(f32[4,64,128]{2,1,0:T(8,128)} %broadcast_in_dim.84), calls=%async_computation | async-start | bytes 262144 | tf_op jit(solution)/shard_map/all_to_all | solution.py:18
  64.0 0.7 multiply_bitcast_fusion
  64.9 0.1 lt.61
  65.0 0.9 reshape.308
  65.9 0.7 iota_compare_fusion.1
  66.6 0.1 fusion.39
  66.7 2.1 %all-to-all-done = f32[4,64,128]{2,1,0:T(8,128)S(1)} async-done(((f32[4,64,128]{2,1,0:T(8,128)}), f32[4,64,128]{2,1,0:T(8,128)S(1)}, u32[]{:S(2)}, u32[]{:S(2)}) %all-to-all-start) | async-done | bytes 131104 | tf_op jit(solution)/shard_map/all_to_all | solution.py:18
  68.8 1.2 fusion.17
  70.1 0.4 fusion.40
  70.4 0.4 fusion.25
  70.8 0.2 convolution_bitcast_fusion
  71.1 19.3 %all-gather.2.cloned.1.call-done = bf16[16,16,16,512]{3,2,1,0:T(8,128)(2,1)} async-done(((bf16[16,2,16,512]{3,2,1,0:T(8,128)(2,1)}), bf16[16,16,16,512]{3,2,1,0:T(8,128)(2,1)}) %all-gather.2.cloned.1.call-update) | async-done | bytes 4194320 | tf_op jit(solution)/shard_map/all_gather | solution.py:93
  90.3 6.9 %reshape_transpose_reshape.3 = bf16[1,4096,2,2,128]{4,3,2,1,0:T(2,128)(2,1)} reshape(bf16[16,16,16,512]{3,2,1,0:T(8,128)(2,1)} %all-gather.2.cloned.1.call-done) | data formatting | bytes 8388608 | tf_op jit(solution)/shard_map/reshape;transpose;reshape | solution.py:97
  97.2 9.0 %fusion.38 = (bf16[1,4096,2,1,128]{4,3,2,1,0:T(2,128)(2,1)S(1)}, bf16[1,4096,2,1,128]{4,3,2,1,0:T(2,128)(2,1)S(1)}) fusion(bf16[1,4096,2,2,128]{4,3,2,1,0:T(2,128)(2,1)} %reshape_transpose_reshape.3), kind=kLoop, calls=%fused_computation.56 | loop fusion | bytes 8388608 | tf_op jit(solution)/shard_map/slice | solution.py:109
  106.2 2.9 %fusion.1 = (f32[2,8,64]{1,2,0:T(8,128)S(1)}, f32[2,64,8,4096]{3,2,1,0:T(8,128)S(1)}) fusion(pred[4096]{0:T(1024)(128)(4,1)S(1)} %lt.61, bf16[1,4096,2,1,128]{4,3,2,1,0:T(2,128)(2,1)S(1)} %get-tuple-element.7, bf16[64,2,8,128]{3,2,1,0:T(8,128)(2,1)S(1)} %bitcast.143), kind=kOutput, calls=%fused_computation.3 | convolution fusion | flops 1086323712 | bytes 19144704 | tf_op jit(solution)/shard_map/bnkgd,blkd->bkgnl/dot_general | solution.py:106
  109.2 4.9 %fusion.2 = f32[2,8,64]{1,2,0:T(8,128)S(1)} fusion(f32[2,64,8,4096]{3,2,1,0:T(8,128)S(1)} %get-tuple-element.16, f32[2,8,64]{1,2,0:T(8,128)S(1)} %max.17, pred[4096]{0:T(1024)(128)(4,1)S(1)} %lt.61), kind=kLoop, calls=%fused_computation.4 | loop fusion | flops 20970496 | bytes 16789504 | tf_op jit(solution)/shard_map/reduce_sum | solution.py:118
  114.1 4.8 %fusion.21 = f32[1,64,2,8,128]{4,3,1,2,0:T(8,128)} fusion(bf16[1,4096,2,1,128]{4,3,2,1,0:T(2,128)(2,1)S(1)} %get-tuple-element.8, f32[2,64,8,4096]{3,2,1,0:T(8,128)S(1)} %get-tuple-element.16, f32[2,8,64]{1,2,0:T(8,128)S(1)} %max.17, pred[4096]{0:T(1024)(128)(4,1)S(1)} %lt.61, f32[2,8,64,128]{3,2,1,0:T(8,128)S(1)} %bitcast.146, ...), kind=kOutput, calls=%fused_computation.23 | convolution fusion | flops 1095106560 | bytes 19939328 | tf_op jit(solution)/shard_map/bkgnl,blkd->bkgnd/dot_general | solution.py:119
  118.9 1.1 copy.38
  120.0 0.5 fusion.24
  120.5 0.9 copy.39
  (16 shorter events, 0.4 us)
Async XLA Ops:
  6.5 62.3 %copy-start = (bf16[128,2048]{1,0:T(8,128)(2,1)S(1)}, bf16[128,2048]{1,0:T(8,128)(2,1)}, u32[]{:S(2)}) copy-start(bf16[128,2048]{1,0:T(8,128)(2,1)} %param.15) | copy-start | bytes 1572868
  6.5 83.8 %all-gather.2.cloned.1.call-start = ((), (), s32[]{:S(2)}) async-start(), calls=%async_computation.2 | async-start | bytes 4718592 | tf_op jit(solution)/shard_map/all_gather | solution.py:93
  54.9 13.9 %all-to-all-start = ((f32[4,64,128]{2,1,0:T(8,128)}), f32[4,64,128]{2,1,0:T(8,128)S(1)}, u32[]{:S(2)}, u32[]{:S(2)}) async-start(f32[4,64,128]{2,1,0:T(8,128)} %broadcast_in_dim.84), calls=%async_computation | async-start | bytes 262144 | tf_op jit(solution)/shard_map/all_to_all | solution.py:18
Sparse Core Ops, SparseCore 0:
  52.2 38.0 all-gather.1
where the time goes:
time: 129 us; the launch traced here: 128 us
  blocking collectives  45.5 us (35%)
  waiting for transfers between devices  21.4 us (17%)
  local copies, waits for them, and re-layouts  20.4 us (16%)
  between operations  13.5 us (10%)
  matrix products  10.8 us (8%)
  starting transfers between devices  9.1 us (7%)
  other arithmetic  7.44 us (6%)
    all_to_all x1, blocking collectives, per_device(): lax.all_to_all(visual_key_value, 'enc', split_axis=0, concat_axis=0, tile...  45.5 us
    all_gather x1, waiting for transfers between devices, per_device(): key_piece = lax.all_gather(exchanged, 'seq', axis=1, tiled=True)  19.3 us
    all_to_all x1, starting transfers between devices, sent_to_all(): return lax.all_to_all(copies, axis, split_axis=0, concat_axis=0, tiled=True)  9.1 us
    slice x1, local copies, waits for them, and re-layouts, per_device(): key_values[:, :, :, 0, :]  8.97 us
    another operation x1, local copies, waits for them, and re-layouts, per_device(): jnp.moveaxis(key_values, 1, 0)  6.92 us
    reduce_sum x1, other arithmetic, per_device(): totals_next = totals_now * rescale + weights.sum(axis=-1)  4.91 us
    dot_general x1, matrix products, per_device(): jnp.einsum('bkgnl,blkd->bkgnd', weights.astype(jnp.bfloat16), key_values[...  4.77 us
    dot_general x1, matrix products, per_device(): jnp.einsum('bnkgd,blkd->bkgnl', query_matrix, key_values[:, :, :, 0, :],...  2.92 us
  transfers between devices with their start and end apart: 2, of which 2 were waited for; matrix products, arithmetic and copies ran while one was open for 6% of the time, Pallas kernels for 0%

commit v1 on v0

v1 whole, which is shorter than its diff:
```python
import math

import jax
import jax.numpy as jnp
from jax import lax
from jax.experimental import pallas as pl
from jax.experimental.pallas import tpu as pltpu
from jax.sharding import PartitionSpec as P

MESH = pl.DeviceIdType.MESH
HEAD_SIZE = 128
ADAPTER_RANK = 16
ADAPTER_SCALE = 2.0
NEG_BIG = -1e30
NX, NZ, NY = 4, 4, 4
SLOTS = NX * NZ
GROUP = 4
KEYS = GROUP * 64
COLS = 1024
BLOCK = 256
EXP2_SCALE = math.log2(math.e) / math.sqrt(HEAD_SIZE)
OFFSETS = (
    [(0, 0), (1, 0), (3, 0), (2, 0)]
    + [(dx, dz) for dx in (2, 3, 1, 0) for dz in (1, 3)]
    + [(dx, 2) for dx in (2, 3, 1, 0)]
)


def spread(rows):
    for shift in (64, 32, 16):
        rows = rows + pltpu.roll(rows, shift, 1)
    return rows


def kernel(
    blocks_ref,
    adapter_ref,
    length_ref,
    visual,
    queries,
    suffix,
    hidden,
    down,
    up,
    out,
    kv,
    sx,
    qx,
    qfull,
    qt,
    acc,
    peak,
    total,
    res,
    hidden_v,
    down_v,
    up_v,
    queries_v,
    tp_send,
    tp_recv,
    len_tile,
    source_of,
    load_sem,
    a2a_send,
    a2a_recv,
    y_send,
    y_recv,
    tp_ssem,
    tp_rsem,
    sib_ssem,
    sib_rsem,
    out_sem,
):
    e, s, t = lax.axis_index("enc"), lax.axis_index("seq"), lax.axis_index("tp")
    x, z = e // NZ, e % NZ
    y, c = s // 2, s % 2
    oc = 1 - c

    def enc_at(dx, dz):
        return ((x + dx) % NX) * NZ + (z + dz) % NZ

    def y_at(dy):
        return (e, ((y + dy) % NY) * 2 + c, t)

    sibling = (e, y * 2 + oc, t)

    loads = [
        pltpu.make_async_copy(src, dst, load_sem.at[i])
        for i, (src, dst) in enumerate(
            ((hidden, hidden_v), (down, down_v), (up, up_v), (queries, queries_v))
        )
    ]
    for load in loads:
        load.start()
    own_cols = pl.ds(pl.multiple_of(c * 256, 256), 256)
    sib_cols = pl.ds(pl.multiple_of(oc * 256, 256), 256)
    own_tile = pltpu.make_async_copy(
        visual.at[e, :, :, own_cols], kv.at[0, 0, pl.ds(2 * c, 2)], load_sem.at[4]
    )
    own_tile.start()
    own_suffix = pltpu.make_async_copy(
        suffix.at[:, :, own_cols], sx.at[c], load_sem.at[5]
    )
    own_suffix.start()

    barrier = pltpu.get_barrier_semaphore()
    peers = [sibling, y_at(1), y_at(3)]
    peers += [(e, s, (t + k) % 4) for k in (1, 2, 3)]
    for dx, dz in OFFSETS[1:]:
        for core in (c, oc):
            peers.append((enc_at(dx, dz), y * 2 + core, t))
    for peer in peers:
        pl.semaphore_signal(barrier, inc=1, device_id=peer, device_id_type=MESH)

    for j, (dx, dz) in enumerate(OFFSETS):
        source_of[j] = enc_at(NX - dx, NZ - dz)

    lane = lax.broadcasted_iota(jnp.int32, (8, 128), 1)
    loads[0].wait()
    loads[1].wait()
    lowered = jnp.dot(hidden_v[...], down_v[...], preferred_element_type=jnp.float32)
    packed = jnp.zeros((8, 128), jnp.float32)
    for g in range(8):
        own_adapter = adapter_ref[0, g // 4]
        rows = jnp.where(lane // ADAPTER_RANK == own_adapter, lowered[8 * g : 8 * g + 8], 0.0)
        packed = jnp.where(lane // ADAPTER_RANK == g, spread(rows), packed)
    tp_send[...] = packed
    len_tile[c] = jnp.where((lane // 32) % 2 == 0, length_ref[0, 0], length_ref[0, 1]).astype(
        jnp.float32
    )

    pl.semaphore_wait(barrier, len(peers))

    def remote(src, dst, ssem, rsem, device):
        return pltpu.make_async_remote_copy(
            src_ref=src,
            dst_ref=dst,
            send_sem=ssem,
            recv_sem=rsem,
            device_id=device,
            device_id_type=MESH,
        )

    tp_copies = [
        remote(
            tp_send, tp_recv.at[k - 1], tp_ssem.at[k - 1], tp_rsem.at[k - 1], (e, s, (t + k) % 4)
        )
        for k in (1, 2, 3)
    ]
    for copy in tp_copies:
        copy.start()

    def tile_send(j, core, cols):
        target = enc_at(*OFFSETS[j])
        return remote(
            visual.at[target, :, :, cols],
            kv.at[0, j, pl.ds(2 * c, 2)],
            a2a_send.at[j, core],
            a2a_recv.at[j, c],
            (target, y * 2 + core, t),
        )

    tile_send(0, oc, sib_cols).start()
    suffix_copy = remote(
        suffix.at[:, :, sib_cols], sx.at[c], sib_ssem.at[0], sib_rsem.at[0], sibling
    )
    suffix_copy.start()
    len_copy = remote(len_tile.at[c], len_tile.at[c], sib_ssem.at[1], sib_rsem.at[1], sibling)
    len_copy.start()
    for j in range(1, SLOTS):
        tile_send(j, c, own_cols).start()
        tile_send(j, oc, sib_cols).start()

    def tile_wait(j, core):
        dst = kv.at[0, j, pl.ds(2 * core, 2)]
        remote(dst, dst, a2a_send.at[j, core], a2a_recv.at[j, core], sibling).wait_recv()

    def y_copy(way, j):
        return remote(
            kv.at[0, j],
            kv.at[1 + way, j],
            y_send.at[way, j],
            y_recv.at[way, j],
            y_at(1 if way == 0 else 3),
        )

    def y_relay(j):
        way = j % 2
        return remote(
            kv.at[1 + way, j],
            kv.at[3, j],
            y_send.at[2, j],
            y_recv.at[2, j],
            (e, ((y + 1 + 2 * way) % NY) * 2 + c, t),
        )

    def y_wait(way, j):
        dst = kv.at[1 + way, j]
        remote(dst, dst, y_send.at[way, j], y_recv.at[way, j], sibling).wait_recv()

    def forward(j):
        y_copy(0, j).start()
        y_copy(1, j).start()

    def relay(j):
        y_wait(j % 2, j)
        y_relay(j).start()

    own_tile.wait()
    tile_wait(0, oc)
    forward(0)

    for copy in tp_copies:
        copy.wait_recv()
    packed = tp_send[...] + tp_recv[0] + tp_recv[1] + tp_recv[2]
    picked = []
    for g in range(8):
        own_adapter = adapter_ref[0, g // 4]
        rows = spread(jnp.where(lane // ADAPTER_RANK == g, packed, 0.0))
        picked.append(jnp.where(lane // ADAPTER_RANK == own_adapter, rows, 0.0))
    picked = jnp.concatenate(picked, axis=0).astype(jnp.bfloat16)
    loads[2].wait()
    loads[3].wait()
    for n in range(8):
        at = slice(n * 256, (n + 1) * 256)
        raised = jnp.dot(picked, up_v[:, at], preferred_element_type=jnp.float32)
        qfull[:, at] = (
            queries_v[:, at].astype(jnp.float32) + ADAPTER_SCALE * raised
        ).astype(jnp.bfloat16)
    own_half = pl.ds(pl.multiple_of(c * COLS, COLS), COLS)
    sib_half = pl.ds(pl.multiple_of(oc * COLS, COLS), COLS)
    query_copy = remote(
        qfull.at[:, sib_half], qx.at[c], sib_ssem.at[2], sib_rsem.at[2], sibling
    )
    query_copy.start()
    qx[c] = qfull[:, own_half]

    for j in range(1, GROUP):
        tile_wait(j, 0)
        tile_wait(j, 1)
        forward(j)
    for j in range(2):
        relay(j)

    for index, dst in ((0, sx.at[oc]), (1, len_tile.at[oc]), (2, qx.at[oc])):
        remote(dst, dst, sib_ssem.at[index], sib_rsem.at[index], sibling).wait_recv()
    own_suffix.wait()

    for g in range(8):
        rows = qx[:, :, g * 128 : (g + 1) * 128].reshape(128, 128)
        qt[:, g * 128 : (g + 1) * 128] = rows.T

    lengths = jnp.where(lane // 64 == 0, len_tile[0], len_tile[1])[0:1].astype(jnp.int32)
    key_at = lax.broadcasted_iota(jnp.int32, (128, 128), 0)
    col_at = lax.broadcasted_iota(jnp.int32, (128, 128), 1)
    limit = jnp.minimum(col_at % 32, lengths - 1)
    seen = (key_at // 32 == col_at // 32) & (key_at % 32 <= limit)
    keys = sx[:, :, :, 0:128].reshape(128, 128)
    values_t = sx[:, :, :, 128:256].reshape(128, 128).T
    for g in range(8):
        at = slice(g * 128, (g + 1) * 128)
        scores = jnp.dot(keys, qt[:, at], preferred_element_type=jnp.float32)
        scores = jnp.where(seen, scores, NEG_BIG)
        top = scores.max(axis=0, keepdims=True)
        weights = jnp.where(seen, jnp.exp2((scores - top) * EXP2_SCALE), 0.0)
        peak[:, at] = top
        total[:, at] = weights.sum(axis=0, keepdims=True)
        acc[:, at] = jnp.dot(
            values_t, weights.astype(jnp.bfloat16), preferred_element_type=jnp.float32
        )

    def attend(r, g):
        tile = kv.at[r, pl.ds(g * GROUP, GROUP)]
        keys = tile[:, :, :, 0:128].reshape(KEYS, 128)
        values_t = tile[:, :, :, 128:256].reshape(KEYS, 128).T
        from_y = (y + jnp.where(r == 0, 0, jnp.where(r == 1, 3, jnp.where(r == 2, 1, 2)))) % NY
        bias = []
        for i in range(GROUP * 4):
            held = blocks_ref[0, from_y * 4 + i % 4]
            live = source_of[g * GROUP + i // 4] < 2 * held
            bias.append(jnp.where(live, 0.0, NEG_BIG))
        for b in range(COLS // BLOCK):
            at = slice(b * BLOCK, (b + 1) * BLOCK)
            scores = jnp.dot(keys, qt[:, at], preferred_element_type=jnp.float32)
            before = peak[:, at]
            top = before
            for i in range(GROUP * 4):
                part = scores[16 * i : 16 * i + 16].max(axis=0, keepdims=True)
                top = jnp.maximum(top, part + bias[i])
            shrink = jnp.exp2((before - top) * EXP2_SCALE)
            parts = []
            added = jnp.zeros((16, BLOCK), jnp.float32)
            for i in range(GROUP * 4):
                part = jnp.exp2((scores[16 * i : 16 * i + 16] - (top - bias[i])) * EXP2_SCALE)
                added = added + part
                parts.append(part.astype(jnp.bfloat16))
            peak[:, at] = top
            total[:, at] = total[:, at] * shrink + added.sum(axis=0, keepdims=True)
            acc[:, at] = acc[:, at] * shrink + jnp.dot(
                values_t, jnp.concatenate(parts, axis=0), preferred_element_type=jnp.float32
            )

    def step(k, _):
        @pl.when(k < SLOTS)
        def _():
            tile_wait(k, 0)
            tile_wait(k, 1)
            forward(k)

        @pl.when(k < SLOTS + 2)
        def _():
            relay(k - 2)

        unit = k - GROUP
        g, r = unit // 4, unit % 4
        for i in range(GROUP):
            j = g * GROUP + i

            @pl.when((r == 1 + (1 - i % 2)) | (r == 3))
            def _():
                way = jnp.where(r == 3, 2, 1 - i % 2)
                y_wait(way, j)

        attend(r, g)
        return 0

    lax.fori_loop(GROUP, SLOTS + GROUP, step, 0)

    keep = lax.broadcasted_iota(jnp.int32, (1, 128), 1) % 32 < lengths
    for g in range(8):
        at = slice(g * 128, (g + 1) * 128)
        rows = jnp.where(keep, acc[:, at] / total[:, at], 0.0).T
        res[:, :, at] = rows.reshape(2, 64, 128).astype(jnp.bfloat16)
    out_copy = remote(
        res.at[oc], out.at[:, own_half], sib_ssem.at[3], sib_rsem.at[3], sibling
    )
    out_copy.start()
    local_out = pltpu.make_async_copy(res.at[c], out.at[:, own_half], out_sem)
    local_out.start()

    def drain(j, _):
        for core in (0, 1):

            @pl.when((j > 0) | (core == oc))
            def _():
                src = kv.at[0, j, pl.ds(2 * core, 2)]
                remote(src, src, a2a_send.at[j, core], a2a_recv.at[j, core], sibling).wait_send()

        for way in (0, 1, 2):
            src = kv.at[1 + way, j]
            remote(src, src, y_send.at[way, j], y_recv.at[way, j], sibling).wait_send()
        return 0

    lax.fori_loop(0, SLOTS, drain, 0)
    for copy in tp_copies + [suffix_copy, len_copy, query_copy]:
        copy.wait_send()
    local_out.wait()
    out_copy.wait_send()
    arrived = out.at[:, sib_half]
    remote(arrived, arrived, sib_ssem.at[3], sib_rsem.at[3], sibling).wait_recv()


def per_device(
    visual_key_value,
    patch_blocks,
    queries,
    suffix_key_value,
    suffix_hidden_state,
    down_weight,
    up_weight,
    question_adapter,
    suffix_token_length,
):
    bf16, f32 = jnp.bfloat16, jnp.float32
    asked, positions, width = queries.shape[1:]
    rows = asked * positions
    dma = pltpu.SemaphoreType.DMA
    smem = pl.BlockSpec(memory_space=pltpu.SMEM)
    hbm = pl.BlockSpec(memory_space=pl.ANY)
    result = pl.pallas_call(
        kernel,
        name="attention",
        out_shape=jax.ShapeDtypeStruct((rows, width), bf16),
        in_specs=[smem] * 3 + [hbm] * 6,
        out_specs=hbm,
        scratch_shapes=[
            pltpu.VMEM((4, SLOTS, 4, 16, 256), bf16),
            pltpu.VMEM((2, 2, 32, 256), bf16),
            pltpu.VMEM((2, rows, COLS), bf16),
            pltpu.VMEM((rows, width), bf16),
            pltpu.VMEM((HEAD_SIZE, COLS), bf16),
            pltpu.VMEM((HEAD_SIZE, COLS), f32),
            pltpu.VMEM((1, COLS), f32),
            pltpu.VMEM((1, COLS), f32),
            pltpu.VMEM((2, rows, COLS), bf16),
            pltpu.VMEM((rows, width), bf16),
            pltpu.VMEM(down_weight.shape, bf16),
            pltpu.VMEM(up_weight.shape, bf16),
            pltpu.VMEM((rows, width), bf16),
            pltpu.VMEM((8, 128), f32),
            pltpu.VMEM((3, 8, 128), f32),
            pltpu.VMEM((2, 8, 128), f32),
            pltpu.SMEM((SLOTS,), jnp.int32),
            dma((6,)),
            dma((SLOTS, 2)),
            dma((SLOTS, 2)),
            dma((3, SLOTS)),
            dma((3, SLOTS)),
            dma((3,)),
            dma((3,)),
            dma((4,)),
            dma((4,)),
            dma,
        ],
        compiler_params=pltpu.CompilerParams(
            collective_id=0, has_side_effects=True, vmem_limit_bytes=56 << 20
        ),
    )(
        patch_blocks,
        question_adapter,
        suffix_token_length,
        visual_key_value,
        queries.reshape(rows, width),
        suffix_key_value.reshape(asked, positions, -1),
        suffix_hidden_state.reshape(rows, width),
        down_weight,
        up_weight,
    )
    return result.reshape(queries.shape)


def solution(mesh):
    placed = (
        P(None, "seq", "enc", "tp"),
        P("enc", None),
        P("enc", "seq", None, "tp"),
        P("enc", "seq", None, "tp"),
        P("enc", "seq", None, "tp"),
        P("tp", None),
        P(None, "tp"),
        P("enc", "seq"),
        P("enc", "seq"),
    )
    return jax.shard_map(
        per_device,
        mesh=mesh,
        in_specs=placed,
        out_specs=P("enc", "seq", None, "tp"),
        check_vma=False,
    )
```

time: 129 us -> 59.8 us (0.46)
  Pallas kernels: 0 us -> 57.9 us
  blocking collectives: 45.5 us -> 0 us
  waiting for transfers between devices: 21.4 us -> 0 us
  local copies, waits for them, and re-layouts: 20.4 us -> 1.67 us
  between operations: 13.5 us -> 0.01 us
  matrix products: 10.8 us -> 0 us
  starting transfers between devices: 9.1 us -> 0 us
  other arithmetic: 7.44 us -> 0 us
    pallas_call x0 -> x1, Pallas kernels: none -> 57.9 us  [per_device(): pl.pallas_call(kernel, name='attention', out_shape=jax.ShapeDtypeStruct((...]
    all_to_all x1 -> x0, blocking collectives: 45.5 us -> none  [per_device(): lax.all_to_all(visual_key_value, 'enc', split_axis=0, concat_axis=0, tile...]
    all_gather x1 -> x0, waiting for transfers between devices: 19.3 us -> none  [per_device(): key_piece = lax.all_gather(exchanged, 'seq', axis=1, tiled=True)]
    dot_general x6 -> x0, matrix products: 10.8 us -> none  [the longest x1 4.77 us: per_device(): jnp.einsum('bkgnl,blkd->bkgnd', weights.astype(jnp.bfloat16), key_values[...]
    all_to_all x1 -> x0, starting transfers between devices: 9.1 us -> none  [sent_to_all(): return lax.all_to_all(copies, axis, split_axis=0, concat_axis=0, tiled=True)]
    slice x2 -> x0, local copies, waits for them, and re-layouts: 9.07 us -> none  [the longest x1 8.97 us: per_device(): key_values[:, :, :, 0, :]]
    another operation x1 -> x0, local copies, waits for them, and re-layouts: 6.92 us -> none  [per_device(): jnp.moveaxis(key_values, 1, 0)]
    reduce_sum x3 -> x0, other arithmetic: 5.31 us -> none  [the longest x1 4.91 us: per_device(): totals_next = totals_now * rescale + weights.sum(axis=-1)]
  transfers between devices with their start and end apart: 2 -> 0, of which waited for: 2 -> 0; matrix products, arithmetic and copies ran while one was open for 6% -> 0% of each run, Pallas kernels for 0% -> 0%
where the time goes in v1:
time: 59.8 us; the launch traced here: 59.6 us
  Pallas kernels  57.9 us (97%)
  local copies, waits for them, and re-layouts  1.67 us (3%)
    pallas_call x1, Pallas kernels, per_device(): pl.pallas_call(kernel, name='attention', out_shape=jax.ShapeDtypeStruct((...  57.9 us
    unnamed x1, local copies, waits for them, and re-layouts  1.67 us

profile of v1, /device:TPU:1, one launch (start us, length us, event | category | flops | bytes accessed | tf_op | source)
XLA Modules:
  0.0 59.6 jit_solution(1708540910700782813)
XLA Ops:
  0.0 57.9 %attention.1 = bf16[64,2048]{1,0:T(8,128)(2,1)} custom-call(s32[1,16]{1,0:T(1,128)} %blocks_ref.1, s32[1,2]{1,0:T(1,128)} %adapter_ref.1, s32[1,2]{1,0:T(1,128)} %length_ref.1, bf16[16,2,16,512]{3,2,1,0:T(8,128)(2,1)} %visual.1, bf16[64,2048]{1,0:T(8,128)(2,1)} %bitcast.5, bf16[2,32,512]{2,1,0:T(8,128)(2,1)} %bitcast.7, bf16[64,2048]{1,0:T(8,128)(2,1)} %bitcast.6, ...), custom_call_target="tpu_custom_call" | custom-call | tf_op jit(solution)/shard_map/attention/pallas_call | solution.py:380
  57.9 1.7 %copy.11 = bf16[1,2,32,2048]{3,2,1,0:T(8,128)(2,1)} copy(bf16[1,2,32,2048]{3,2,1,0:T(8,128)(2,1)} %bitcast.4) | data formatting | bytes 524288

commit v2 on v1

--- a/solution.py
+++ b/solution.py
@@ -17,13 +17,14 @@
 GROUP = 4
 KEYS = GROUP * 64
 COLS = 1024
-BLOCK = 256
+BLOCK = 128
 EXP2_SCALE = math.log2(math.e) / math.sqrt(HEAD_SIZE)
-OFFSETS = (
-    [(0, 0), (1, 0), (3, 0), (2, 0)]
-    + [(dx, dz) for dx in (2, 3, 1, 0) for dz in (1, 3)]
-    + [(dx, 2) for dx in (2, 3, 1, 0)]
-)
+HERE = [(0, 0), (1, 0), (3, 0), (2, 0)]
+NEAR = [(dx, dz) for dx in (2, 3, 1, 0) for dz in (1, 3)]
+FAR = [(dx, 2) for dx in (2, 3, 1, 0)]
+OFFSETS = HERE + NEAR + FAR
+FIRST_FAR = len(HERE + NEAR)
+LATE = GROUP + 1
 
 
 def spread(rows):
@@ -33,9 +34,9 @@
 
 
 def kernel(
-    blocks_ref,
-    adapter_ref,
-    length_ref,
+    blocks,
+    adapter,
+    length,
     visual,
     queries,
     suffix,
@@ -60,6 +61,9 @@
     tp_recv,
     len_tile,
     source_of,
+    blocks_ref,
+    adapter_ref,
+    length_ref,
     load_sem,
     a2a_send,
     a2a_recv,
@@ -69,7 +73,9 @@
     tp_rsem,
     sib_ssem,
     sib_rsem,
-    out_sem,
+    out_ssem,
+    out_rsem,
+    far_ready,
 ):
     e, s, t = lax.axis_index("enc"), lax.axis_index("seq"), lax.axis_index("tp")
     x, z = e // NZ, e % NZ
@@ -84,6 +90,15 @@
 
     sibling = (e, y * 2 + oc, t)
 
+    barrier = pltpu.get_barrier_semaphore()
+    peers = [sibling, y_at(1), y_at(2), y_at(3)]
+    peers += [(e, s, (t + k) % 4) for k in (1, 2, 3)]
+    for dx, dz in (HERE + NEAR)[1:]:
+        for core in (c, oc):
+            peers.append((enc_at(dx, dz), y * 2 + core, t))
+    for peer in peers:
+        pl.semaphore_signal(barrier, inc=1, device_id=peer, device_id_type=MESH)
+
     loads = [
         pltpu.make_async_copy(src, dst, load_sem.at[i])
         for i, (src, dst) in enumerate(
@@ -91,6 +106,14 @@
         )
     ]
     for load in loads:
+        load.start()
+    scalars = [
+        pltpu.make_async_copy(src, dst, load_sem.at[6 + i])
+        for i, (src, dst) in enumerate(
+            ((blocks, blocks_ref), (adapter, adapter_ref), (length, length_ref))
+        )
+    ]
+    for load in scalars:
         load.start()
     own_cols = pl.ds(pl.multiple_of(c * 256, 256), 256)
     sib_cols = pl.ds(pl.multiple_of(oc * 256, 256), 256)
@@ -103,21 +126,12 @@
     )
     own_suffix.start()
 
-    barrier = pltpu.get_barrier_semaphore()
-    peers = [sibling, y_at(1), y_at(3)]
-    peers += [(e, s, (t + k) % 4) for k in (1, 2, 3)]
-    for dx, dz in OFFSETS[1:]:
-        for core in (c, oc):
-            peers.append((enc_at(dx, dz), y * 2 + core, t))
-    for peer in peers:
-        pl.semaphore_signal(barrier, inc=1, device_id=peer, device_id_type=MESH)
-
     for j, (dx, dz) in enumerate(OFFSETS):
         source_of[j] = enc_at(NX - dx, NZ - dz)
 
     lane = lax.broadcasted_iota(jnp.int32, (8, 128), 1)
-    loads[0].wait()
-    loads[1].wait()
+    for load in [loads[0], loads[1], *scalars]:
+        load.wait()
     lowered = jnp.dot(hidden_v[...], down_v[...], preferred_element_type=jnp.float32)
     packed = jnp.zeros((8, 128), jnp.float32)
     for g in range(8):
@@ -150,8 +164,8 @@
     for copy in tp_copies:
         copy.start()
 
-    def tile_send(j, core, cols):
-        target = enc_at(*OFFSETS[j])
+    def tile_send(dx, dz, j, core, cols):
+        target = enc_at(dx, dz)
         return remote(
             visual.at[target, :, :, cols],
             kv.at[0, j, pl.ds(2 * c, 2)],
@@ -160,16 +174,29 @@
             (target, y * 2 + core, t),
         )
 
-    tile_send(0, oc, sib_cols).start()
+    tile_send(0, 0, 0, oc, sib_cols).start()
     suffix_copy = remote(
         suffix.at[:, :, sib_cols], sx.at[c], sib_ssem.at[0], sib_rsem.at[0], sibling
     )
     suffix_copy.start()
     len_copy = remote(len_tile.at[c], len_tile.at[c], sib_ssem.at[1], sib_rsem.at[1], sibling)
     len_copy.start()
-    for j in range(1, SLOTS):
-        tile_send(j, c, own_cols).start()
-        tile_send(j, oc, sib_cols).start()
+    for j in range(1, GROUP):
+        tile_send(*OFFSETS[j], j, c, own_cols).start()
+        tile_send(*OFFSETS[j], j, oc, sib_cols).start()
+    for j in range(GROUP, FIRST_FAR):
+        tile_send(*OFFSETS[j], j, c, own_cols).start()
+        tile_send(*OFFSETS[j], j, oc, sib_cols).start()
+    pl.semaphore_signal(
+        far_ready, inc=1, device_id=(enc_at(0, NZ - 1), s, t), device_id_type=MESH
+    )
+
+    def far_sends():
+        for j in range(FIRST_FAR, SLOTS):
+            tile_send(*OFFSETS[j], j, c, own_cols).start()
+            tile_send(*OFFSETS[j], j, oc, sib_cols).start()
+
+    inner = (t == 1) | (t == 2)
 
     def tile_wait(j, core):
         dst = kv.at[0, j, pl.ds(2 * core, 2)]
@@ -194,6 +221,11 @@
             (e, ((y + 1 + 2 * way) % NY) * 2 + c, t),
         )
 
+    def y_across(j):
+        return remote(
+            kv.at[0, j], kv.at[3, j], y_send.at[2, j], y_recv.at[2, j], y_at(2)
+        )
+
     def y_wait(way, j):
         dst = kv.at[1 + way, j]
         remote(dst, dst, y_send.at[way, j], y_recv.at[way, j], sibling).wait_recv()
@@ -209,6 +241,12 @@
     own_tile.wait()
     tile_wait(0, oc)
     forward(0)
+
+    pl.semaphore_wait(far_ready, 1)
+
+    @pl.when(inner)
+    def _():
+        far_sends()
 
     for copy in tp_copies:
         copy.wait_recv()
@@ -283,16 +321,19 @@
             at = slice(b * BLOCK, (b + 1) * BLOCK)
             scores = jnp.dot(keys, qt[:, at], preferred_element_type=jnp.float32)
             before = peak[:, at]
-            top = before
+            top = None
             for i in range(GROUP * 4):
-                part = scores[16 * i : 16 * i + 16].max(axis=0, keepdims=True)
-                top = jnp.maximum(top, part + bias[i])
+                low, high = scores[16 * i : 16 * i + 8], scores[16 * i + 8 : 16 * i + 16]
+                part = jnp.maximum(low, high) + bias[i]
+                top = part if top is None else jnp.maximum(top, part)
+            top = jnp.maximum(before, top.max(axis=0, keepdims=True))
             shrink = jnp.exp2((before - top) * EXP2_SCALE)
+            scaled_top = top * EXP2_SCALE
             parts = []
-            added = jnp.zeros((16, BLOCK), jnp.float32)
+            added = jnp.zeros((8, BLOCK), jnp.float32)
             for i in range(GROUP * 4):
-                part = jnp.exp2((scores[16 * i : 16 * i + 16] - (top - bias[i])) * EXP2_SCALE)
-                added = added + part
+                part = jnp.exp2(scores[16 * i : 16 * i + 16] * EXP2_SCALE - (scaled_top - bias[i]))
+                added = added + (part[:8] + part[8:])
                 parts.append(part.astype(jnp.bfloat16))
             peak[:, at] = top
             total[:, at] = total[:, at] * shrink + added.sum(axis=0, keepdims=True)
@@ -307,7 +348,15 @@
             tile_wait(k, 1)
             forward(k)
 
-        @pl.when(k < SLOTS + 2)
+        @pl.when((k >= FIRST_FAR) & (k < SLOTS))
+        def _():
+            y_across(k).start()
+
+        @pl.when((k == LATE) & jnp.logical_not(inner))
+        def _():
+            far_sends()
+
+        @pl.when(k < FIRST_FAR + 2)
         def _():
             relay(k - 2)
 
@@ -316,9 +365,9 @@
         for i in range(GROUP):
             j = g * GROUP + i
 
-            @pl.when((r == 1 + (1 - i % 2)) | (r == 3))
+            @pl.when((r == 2 - i % 2) | ((r > 0) & (j >= FIRST_FAR)) | (r == 3))
             def _():
-                way = jnp.where(r == 3, 2, 1 - i % 2)
+                way = r - 1
                 y_wait(way, j)
 
         attend(r, g)
@@ -327,16 +376,24 @@
     lax.fori_loop(GROUP, SLOTS + GROUP, step, 0)
 
     keep = lax.broadcasted_iota(jnp.int32, (1, 128), 1) % 32 < lengths
-    for g in range(8):
-        at = slice(g * 128, (g + 1) * 128)
-        rows = jnp.where(keep, acc[:, at] / total[:, at], 0.0).T
-        res[:, :, at] = rows.reshape(2, 64, 128).astype(jnp.bfloat16)
-    out_copy = remote(
-        res.at[oc], out.at[:, own_half], sib_ssem.at[3], sib_rsem.at[3], sibling
-    )
-    out_copy.start()
-    local_out = pltpu.make_async_copy(res.at[c], out.at[:, own_half], out_sem)
-    local_out.start()
+    out_copies = []
+    for n in range(4):
+        for g in (2 * n, 2 * n + 1):
+            at = slice(g * 128, (g + 1) * 128)
+            rows = jnp.where(keep, acc[:, at] * (1.0 / total[:, at]), 0.0)
+            rows = rows.astype(jnp.bfloat16).T
+            res[:, :, at] = rows.reshape(2, 64, 128)
+        half = pl.ds(pl.multiple_of(c * COLS + n * 256, 256), 256)
+        copy = remote(
+            res.at[oc, :, n * 256 : (n + 1) * 256],
+            out.at[:, half],
+            out_ssem.at[n],
+            out_rsem.at[n],
+            sibling,
+        )
+        copy.start()
+        out_copies.append(copy)
+    out[:, own_half] = res[c]
 
     def drain(j, _):
         for core in (0, 1):
@@ -354,10 +411,10 @@
     lax.fori_loop(0, SLOTS, drain, 0)
     for copy in tp_copies + [suffix_copy, len_copy, query_copy]:
         copy.wait_send()
-    local_out.wait()
-    out_copy.wait_send()
-    arrived = out.at[:, sib_half]
-    remote(arrived, arrived, sib_ssem.at[3], sib_rsem.at[3], sibling).wait_recv()
+    for n, copy in enumerate(out_copies):
+        copy.wait_send()
+        arrived = out.at[:, pl.ds(pl.multiple_of(oc * COLS + n * 256, 256), 256)]
+        remote(arrived, arrived, out_ssem.at[n], out_rsem.at[n], sibling).wait_recv()
 
 
 def per_device(
@@ -375,14 +432,13 @@
     asked, positions, width = queries.shape[1:]
     rows = asked * positions
     dma = pltpu.SemaphoreType.DMA
-    smem = pl.BlockSpec(memory_space=pltpu.SMEM)
     hbm = pl.BlockSpec(memory_space=pl.ANY)
     result = pl.pallas_call(
         kernel,
         name="attention",
         out_shape=jax.ShapeDtypeStruct((rows, width), bf16),
-        in_specs=[smem] * 3 + [hbm] * 6,
-        out_specs=hbm,
+        in_specs=[hbm] * 9,
+        out_specs=pl.BlockSpec(memory_space=pltpu.VMEM),
         scratch_shapes=[
             pltpu.VMEM((4, SLOTS, 4, 16, 256), bf16),
             pltpu.VMEM((2, 2, 32, 256), bf16),
@@ -401,16 +457,21 @@
             pltpu.VMEM((3, 8, 128), f32),
             pltpu.VMEM((2, 8, 128), f32),
             pltpu.SMEM((SLOTS,), jnp.int32),
-            dma((6,)),
+            pltpu.SMEM(patch_blocks.shape, jnp.int32),
+            pltpu.SMEM(question_adapter.shape, jnp.int32),
+            pltpu.SMEM(suffix_token_length.shape, jnp.int32),
+            dma((9,)),
             dma((SLOTS, 2)),
             dma((SLOTS, 2)),
             dma((3, SLOTS)),
             dma((3, SLOTS)),
             dma((3,)),
             dma((3,)),
+            dma((3,)),
+            dma((3,)),
             dma((4,)),
             dma((4,)),
-            dma,
+            pltpu.SemaphoreType.REGULAR,
         ],
         compiler_params=pltpu.CompilerParams(
             collective_id=0, has_side_effects=True, vmem_limit_bytes=56 << 20

time: 59.8 us -> 56.1 us (0.938)
  Pallas kernels: 57.9 us -> 54.2 us
    pallas_call x1, Pallas kernels: 57.9 us -> 54.2 us  [per_device(): pl.pallas_call(kernel, name='attention', out_shape=jax.ShapeDtypeStruct((...]
where the time goes in v2:
time: 56.1 us; the launch traced here: 55.9 us
  Pallas kernels  54.2 us (97%)
  local copies, waits for them, and re-layouts  1.67 us (3%)
    pallas_call x1, Pallas kernels, per_device(): pl.pallas_call(kernel, name='attention', out_shape=jax.ShapeDtypeStruct((...  54.2 us
    unnamed x1, local copies, waits for them, and re-layouts  1.67 us

profile of v2, /device:TPU:1, one launch (start us, length us, event | category | flops | bytes accessed | tf_op | source)
XLA Modules:
  0.0 55.9 jit_solution(17645638110443868423)
XLA Ops:
  0.0 54.2 %attention.1 = bf16[64,2048]{1,0:T(8,128)(2,1)} custom-call(s32[1,16]{1,0:T(1,128)} %blocks.1, s32[1,2]{1,0:T(1,128)} %adapter.1, s32[1,2]{1,0:T(1,128)} %length.1, bf16[16,2,16,512]{3,2,1,0:T(8,128)(2,1)} %visual.1, bf16[64,2048]{1,0:T(8,128)(2,1)} %bitcast.5, bf16[2,32,512]{2,1,0:T(8,128)(2,1)} %bitcast.7, bf16[64,2048]{1,0:T(8,128)(2,1)} %bitcast.6, ...), custom_call_target="tpu_custom_call" | custom-call | tf_op jit(solution)/shard_map/attention/pallas_call | solution.py:436
  54.2 1.7 %copy.11 = bf16[1,2,32,2048]{3,2,1,0:T(8,128)(2,1)} copy(bf16[1,2,32,2048]{3,2,1,0:T(8,128)(2,1)} %bitcast.4) | data formatting | bytes 524288

commit v3 on v2

--- a/solution.py
+++ b/solution.py
@@ -25,6 +25,7 @@
 OFFSETS = HERE + NEAR + FAR
 FIRST_FAR = len(HERE + NEAR)
 LATE = GROUP + 1
+HELD = SLOTS - 2
 
 
 def spread(rows):
@@ -76,6 +77,7 @@
     out_ssem,
     out_rsem,
     far_ready,
+    pair_ready,
 ):
     e, s, t = lax.axis_index("enc"), lax.axis_index("seq"), lax.axis_index("tp")
     x, z = e // NZ, e % NZ
@@ -94,8 +96,7 @@
     peers = [sibling, y_at(1), y_at(2), y_at(3)]
     peers += [(e, s, (t + k) % 4) for k in (1, 2, 3)]
     for dx, dz in (HERE + NEAR)[1:]:
-        for core in (c, oc):
-            peers.append((enc_at(dx, dz), y * 2 + core, t))
+        peers.append((enc_at(dx, dz), s, t))
     for peer in peers:
         pl.semaphore_signal(barrier, inc=1, device_id=peer, device_id_type=MESH)
 
@@ -145,6 +146,8 @@
 
     pl.semaphore_wait(barrier, len(peers))
 
+    pl.semaphore_signal(pair_ready, inc=1, device_id=sibling, device_id_type=MESH)
+
     def remote(src, dst, ssem, rsem, device):
         return pltpu.make_async_remote_copy(
             src_ref=src,
@@ -181,10 +184,12 @@
     suffix_copy.start()
     len_copy = remote(len_tile.at[c], len_tile.at[c], sib_ssem.at[1], sib_rsem.at[1], sibling)
     len_copy.start()
-    for j in range(1, GROUP):
+    for j in range(1, GROUP + 2):
         tile_send(*OFFSETS[j], j, c, own_cols).start()
+    pl.semaphore_wait(pair_ready, 1)
+    for j in range(1, GROUP + 2):
         tile_send(*OFFSETS[j], j, oc, sib_cols).start()
-    for j in range(GROUP, FIRST_FAR):
+    for j in range(GROUP + 2, FIRST_FAR):
         tile_send(*OFFSETS[j], j, c, own_cols).start()
         tile_send(*OFFSETS[j], j, oc, sib_cols).start()
     pl.semaphore_signal(
@@ -360,20 +365,22 @@
         def _():
             relay(k - 2)
 
-        unit = k - GROUP
-        g, r = unit // 4, unit % 4
-        for i in range(GROUP):
-            j = g * GROUP + i
-
-            @pl.when((r == 2 - i % 2) | ((r > 0) & (j >= FIRST_FAR)) | (r == 3))
-            def _():
-                way = r - 1
-                y_wait(way, j)
-
-        attend(r, g)
+        @pl.when((k < HELD) | (k >= SLOTS))
+        def _():
+            unit = jnp.where(k < SLOTS, k - GROUP, k - GROUP - (SLOTS - HELD))
+            g, r = unit // 4, unit % 4
+            for i in range(GROUP):
+                j = g * GROUP + i
+
+                @pl.when((r == 2 - i % 2) | ((r > 0) & (j >= FIRST_FAR)) | (r == 3))
+                def _():
+                    y_wait(r - 1, j)
+
+            attend(r, g)
+
         return 0
 
-    lax.fori_loop(GROUP, SLOTS + GROUP, step, 0)
+    lax.fori_loop(GROUP, SLOTS + GROUP + (SLOTS - HELD), step, 0)
 
     keep = lax.broadcasted_iota(jnp.int32, (1, 128), 1) % 32 < lengths
     out_copies = []
@@ -472,6 +479,7 @@
             dma((4,)),
             dma((4,)),
             pltpu.SemaphoreType.REGULAR,
+            pltpu.SemaphoreType.REGULAR,
         ],
         compiler_params=pltpu.CompilerParams(
             collective_id=0, has_side_effects=True, vmem_limit_bytes=56 << 20

time: 56.1 us -> 54.2 us (0.966)
  Pallas kernels: 54.2 us -> 52.4 us
    pallas_call x1, Pallas kernels: 54.2 us -> 52.4 us  [per_device(): pl.pallas_call(kernel, name='attention', out_shape=jax.ShapeDtypeStruct((...]
where the time goes in v3:
time: 54.2 us; the launch traced here: 54 us
  Pallas kernels  52.4 us (97%)
  local copies, waits for them, and re-layouts  1.67 us (3%)
    pallas_call x1, Pallas kernels, per_device(): pl.pallas_call(kernel, name='attention', out_shape=jax.ShapeDtypeStruct((...  52.4 us
    unnamed x1, local copies, waits for them, and re-layouts  1.67 us

profile of v3, /device:TPU:1, one launch (start us, length us, event | category | flops | bytes accessed | tf_op | source)
XLA Modules:
  0.0 54.0 jit_solution(10207666915068854646)
XLA Ops:
  0.0 52.4 %attention.1 = bf16[64,2048]{1,0:T(8,128)(2,1)} custom-call(s32[1,16]{1,0:T(1,128)} %blocks.1, s32[1,2]{1,0:T(1,128)} %adapter.1, s32[1,2]{1,0:T(1,128)} %length.1, bf16[16,2,16,512]{3,2,1,0:T(8,128)(2,1)} %visual.1, bf16[64,2048]{1,0:T(8,128)(2,1)} %bitcast.5, bf16[2,32,512]{2,1,0:T(8,128)(2,1)} %bitcast.7, bf16[64,2048]{1,0:T(8,128)(2,1)} %bitcast.6, ...), custom_call_target="tpu_custom_call" | custom-call | tf_op jit(solution)/shard_map/attention/pallas_call | solution.py:443
  52.4 1.7 %copy.11 = bf16[1,2,32,2048]{3,2,1,0:T(8,128)(2,1)} copy(bf16[1,2,32,2048]{3,2,1,0:T(8,128)(2,1)} %bitcast.4) | data formatting | bytes 524288

commit v4 on v3

--- a/solution.py
+++ b/solution.py
@@ -20,7 +20,7 @@
 BLOCK = 128
 EXP2_SCALE = math.log2(math.e) / math.sqrt(HEAD_SIZE)
 HERE = [(0, 0), (1, 0), (3, 0), (2, 0)]
-NEAR = [(dx, dz) for dx in (2, 3, 1, 0) for dz in (1, 3)]
+NEAR = [(dx, dz) for dx in (0, 1, 3, 2) for dz in (1, 3)]
 FAR = [(dx, 2) for dx in (2, 3, 1, 0)]
 OFFSETS = HERE + NEAR + FAR
 FIRST_FAR = len(HERE + NEAR)

time: 54.2 us -> 53 us (0.978); the launches traced: 54 us -> 52.1 us
  Pallas kernels: 52.4 us -> 50.4 us
    pallas_call x1, Pallas kernels: 52.4 us -> 50.4 us  [per_device(): pl.pallas_call(kernel, name='attention', out_shape=jax.ShapeDtypeStruct((...]
where the time goes in v4:
time: 53 us; the launch traced here: 52.1 us
  Pallas kernels  50.4 us (95%)
  local copies, waits for them, and re-layouts  1.67 us (3%)
    pallas_call x1, Pallas kernels, per_device(): pl.pallas_call(kernel, name='attention', out_shape=jax.ShapeDtypeStruct((...  50.4 us
    unnamed x1, local copies, waits for them, and re-layouts  1.67 us

profile of v4, /device:TPU:1, one launch (start us, length us, event | category | flops | bytes accessed | tf_op | source)
XLA Modules:
  0.0 52.1 jit_solution(6219475737807429359)
XLA Ops:
  0.0 50.4 %attention.1 = bf16[64,2048]{1,0:T(8,128)(2,1)} custom-call(s32[1,16]{1,0:T(1,128)} %blocks.1, s32[1,2]{1,0:T(1,128)} %adapter.1, s32[1,2]{1,0:T(1,128)} %length.1, bf16[16,2,16,512]{3,2,1,0:T(8,128)(2,1)} %visual.1, bf16[64,2048]{1,0:T(8,128)(2,1)} %bitcast.5, bf16[2,32,512]{2,1,0:T(8,128)(2,1)} %bitcast.7, bf16[64,2048]{1,0:T(8,128)(2,1)} %bitcast.6, ...), custom_call_target="tpu_custom_call" | custom-call | tf_op jit(solution)/shard_map/attention/pallas_call | solution.py:443
  50.4 1.7 %copy.11 = bf16[1,2,32,2048]{3,2,1,0:T(8,128)(2,1)} copy(bf16[1,2,32,2048]{3,2,1,0:T(8,128)(2,1)} %bitcast.4) | data formatting | bytes 524288

commit v5 on v4

--- a/solution.py
+++ b/solution.py
@@ -76,6 +76,7 @@
     sib_rsem,
     out_ssem,
     out_rsem,
+    kept_sem,
     far_ready,
     pair_ready,
 ):
@@ -383,7 +384,7 @@
     lax.fori_loop(GROUP, SLOTS + GROUP + (SLOTS - HELD), step, 0)
 
     keep = lax.broadcasted_iota(jnp.int32, (1, 128), 1) % 32 < lengths
-    out_copies = []
+    out_copies, kept_copies = [], []
     for n in range(4):
         for g in (2 * n, 2 * n + 1):
             at = slice(g * 128, (g + 1) * 128)
@@ -400,7 +401,11 @@
         )
         copy.start()
         out_copies.append(copy)
-    out[:, own_half] = res[c]
+        kept = pltpu.make_async_copy(
+            res.at[c, :, n * 256 : (n + 1) * 256], out.at[:, half], kept_sem.at[n]
+        )
+        kept.start()
+        kept_copies.append(kept)
 
     def drain(j, _):
         for core in (0, 1):
@@ -418,6 +423,8 @@
     lax.fori_loop(0, SLOTS, drain, 0)
     for copy in tp_copies + [suffix_copy, len_copy, query_copy]:
         copy.wait_send()
+    for kept in kept_copies:
+        kept.wait()
     for n, copy in enumerate(out_copies):
         copy.wait_send()
         arrived = out.at[:, pl.ds(pl.multiple_of(oc * COLS + n * 256, 256), 256)]
@@ -445,7 +452,7 @@
         name="attention",
         out_shape=jax.ShapeDtypeStruct((rows, width), bf16),
         in_specs=[hbm] * 9,
-        out_specs=pl.BlockSpec(memory_space=pltpu.VMEM),
+        out_specs=hbm,
         scratch_shapes=[
             pltpu.VMEM((4, SLOTS, 4, 16, 256), bf16),
             pltpu.VMEM((2, 2, 32, 256), bf16),
@@ -478,6 +485,7 @@
             dma((3,)),
             dma((4,)),
             dma((4,)),
+            dma((4,)),
             pltpu.SemaphoreType.REGULAR,
             pltpu.SemaphoreType.REGULAR,
         ],

time: 53 us -> 52.5 us (level)
  no operation moved by 1% of the time
where the time goes in v5:
time: 52.5 us; the launch traced here: 51.5 us
  Pallas kernels  49.9 us (95%)
  local copies, waits for them, and re-layouts  1.67 us (3%)
    pallas_call x1, Pallas kernels, per_device(): pl.pallas_call(kernel, name='attention', out_shape=jax.ShapeDtypeStruct((...  49.9 us
    unnamed x1, local copies, waits for them, and re-layouts  1.67 us

profile of v5, /device:TPU:1, one launch (start us, length us, event | category | flops | bytes accessed | tf_op | source)
XLA Modules:
  0.0 51.5 jit_solution(5898785527060264420)
XLA Ops:
  0.0 49.9 %attention.1 = bf16[64,2048]{1,0:T(8,128)(2,1)} custom-call(s32[1,16]{1,0:T(1,128)} %blocks.1, s32[1,2]{1,0:T(1,128)} %adapter.1, s32[1,2]{1,0:T(1,128)} %length.1, bf16[16,2,16,512]{3,2,1,0:T(8,128)(2,1)} %visual.1, bf16[64,2048]{1,0:T(8,128)(2,1)} %bitcast.5, bf16[2,32,512]{2,1,0:T(8,128)(2,1)} %bitcast.7, bf16[64,2048]{1,0:T(8,128)(2,1)} %bitcast.6, ...), custom_call_target="tpu_custom_call" | custom-call | tf_op jit(solution)/shard_map/attention/pallas_call | solution.py:450
  49.9 1.7 %copy.11 = bf16[1,2,32,2048]{3,2,1,0:T(8,128)(2,1)} copy(bf16[1,2,32,2048]{3,2,1,0:T(8,128)(2,1)} %bitcast.4) | data formatting | bytes 524288
